TPU v7x, 32 devices: a whole 2x2x4 slice. The times are simulated.
32 devices in a mesh: tok: 4 (over z), seq: 8 (over y, x, core).
Axes of the slice: x: 2, y: 2, z: 4, core: 2. Of those that a mesh axis runs over, the one named last changes fastest.
Arguments:
- keys: bfloat16 [8, 2, 4096, 512], P('seq', None, 'tok'), may hold values from -6 to 6
- values: bfloat16 [8, 2, 4096, 512], P('seq', None, 'tok'), may hold values from -6 to 6
- queries: bfloat16 [8, 2, 4096, 512], P('seq', None, 'tok'), may hold values from -6 to 6
- token_rate: float32 [8, 2, 4096], P('seq', None, 'tok'), may hold values from 0.1 to 1
- valid_count: int32 [8, 2], P('seq'), may hold values from 2048 to 4096
- loss_scale: float32 [1], replicated, may hold values from 128 to 2048
- w_gate: bfloat16 [512, 512], replicated, may hold values from -0.25 to 0.25
- w_up: bfloat16 [512, 512], replicated, may hold values from -0.25 to 0.25
- w_down: bfloat16 [512, 512], replicated, may hold values from -0.25 to 0.25
- out_cotangent: bfloat16 [8, 2, 4096, 512], P('seq', None, 'tok'), may hold values from -0.125 to 0.125
Outputs:
- fast_out: bfloat16 [8, 2, 4096, 512], P('seq', None, 'tok')
- grad_gate: float32 [512, 512], P(None, 'tok')
- grad_up: float32 [512, 512], P(None, 'tok')
- grad_down: float32 [512, 512], P('tok')
- levels: float32 [2, 512], P(None, 'tok')
All inputs are finite; a program needn't handle non-finite values.
Results may differ from a plain program's by a relative error of at most 0.0087.
Values may be sent and summed in bfloat16 or wider, within the bound.
A program may use at most 128 MiB of HBM per device.

v0:
```python
import jax
import jax.numpy as jnp
from jax import lax
from jax.sharding import PartitionSpec as P

momentum_keep = 0.9
step_rate = 3.0
tiny_value = 1e-06


def forward(inputs, gate_w, up_w):
    gate = jnp.dot(inputs, gate_w, preferred_element_type=jnp.float32)
    upper = jnp.dot(inputs, up_w, preferred_element_type=jnp.float32)
    hidden = (jax.nn.silu(gate) * upper).astype(jnp.bfloat16)
    return (gate, upper, hidden)


def backward(inputs, gate, upper, hidden, down_w, cotan):
    first = (((0,), (0,)), ((), ()))
    grad_down = lax.dot_general(hidden, cotan, first, preferred_element_type=jnp.float32)
    back = lax.dot_general(
        cotan, down_w, (((1,), (1,)), ((), ())), preferred_element_type=jnp.float32
    )
    sigma = jax.nn.sigmoid(gate)
    d_upper = (back * gate * sigma).astype(jnp.bfloat16)
    d_gate = (back * upper * sigma * (1.0 + gate * (1.0 - sigma))).astype(jnp.bfloat16)
    grad_gate = lax.dot_general(inputs, d_gate, first, preferred_element_type=jnp.float32)
    grad_up = lax.dot_general(inputs, d_upper, first, preferred_element_type=jnp.float32)
    return (grad_gate, grad_up, grad_down)


def renorm(gate_w, up_w, down_w, gate_n, up_n, down_n):
    gate_w = gate_w * (gate_n / jnp.sqrt(jnp.sum(gate_w * gate_w, axis=0) + tiny_value))
    up_w = up_w * (up_n / jnp.sqrt(jnp.sum(up_w * up_w, axis=0) + tiny_value))
    down_w = down_w * (down_n / jnp.sqrt(jnp.sum(down_w * down_w, axis=1) + tiny_value))[:, None]
    return (gate_w, up_w, down_w)


def own_units(triple, start, piece):
    return (
        lax.dynamic_slice_in_dim(triple[0], start, piece, 1),
        lax.dynamic_slice_in_dim(triple[1], start, piece, 1),
        lax.dynamic_slice_in_dim(triple[2], start, piece, 0),
    )


def per_device(
    keys, values, queries, token_rate, valid_count, loss_scale, w_gate, w_up, w_down, out_cotangent
):
    rows = keys.shape[2]
    blocks = keys.shape[1]
    width = w_gate.shape[1]
    parts = lax.axis_size("tok")
    where = lax.axis_index("tok")
    piece = width // parts
    start = where * piece
    positions = where * rows + jnp.arange(rows, dtype=jnp.int32)
    scale = loss_scale[0]
    gate_full = w_gate.astype(jnp.float32)
    up_full = w_up.astype(jnp.float32)
    down_full = w_down.astype(jnp.float32)
    gate_n = jnp.sqrt(jnp.sum(gate_full * gate_full, axis=0) + tiny_value)
    up_n = jnp.sqrt(jnp.sum(up_full * up_full, axis=0) + tiny_value)
    down_n = jnp.sqrt(jnp.sum(down_full * down_full, axis=1) + tiny_value)
    state = own_units((gate_full, up_full, down_full), start, piece)
    norms = tuple(
        (lax.dynamic_slice_in_dim(entry, start, piece, 0) for entry in (gate_n, up_n, down_n))
    )
    momentum = tuple((jnp.zeros_like(entry) for entry in state))
    totals = (jnp.zeros_like(gate_full), jnp.zeros_like(up_full), jnp.zeros_like(down_full))
    current = (w_gate, w_up, w_down)
    level_list = []
    output_list = []
    for index in range(blocks):
        count = valid_count[0, index]
        mask = (positions < count).astype(jnp.float32)
        inputs = keys[0, index]
        gate, upper, hidden = forward(inputs, current[0], current[1])
        factor = -(scale * token_rate[0, index] * mask / count.astype(jnp.float32))
        cotan = (factor[:, None] * values[0, index].astype(jnp.float32)).astype(jnp.bfloat16)
        grads = backward(inputs, gate, upper, hidden, current[2], cotan)
        summed = (
            lax.psum_scatter(grads[0], "tok", scatter_dimension=1, tiled=True),
            lax.psum_scatter(grads[1], "tok", scatter_dimension=1, tiled=True),
            lax.psum_scatter(grads[2], "tok", scatter_dimension=0, tiled=True),
        )
        level_piece = jnp.max(jnp.abs(summed[0]), axis=0)
        level_list.append(lax.pmax(level_piece, "seq"))
        momentum = tuple(
            (momentum_keep * held + grad / scale for held, grad in zip(momentum, summed))
        )
        stepped = tuple((entry - step_rate * held for entry, held in zip(state, momentum)))
        state = renorm(stepped[0], stepped[1], stepped[2], norms[0], norms[1], norms[2])
        rounded = tuple((entry.astype(jnp.bfloat16) for entry in state))
        current = (
            lax.all_gather(rounded[0], "tok", axis=1, tiled=True),
            lax.all_gather(rounded[1], "tok", axis=1, tiled=True),
            lax.all_gather(rounded[2], "tok", axis=0, tiled=True),
        )
        inputs = queries[0, index]
        gate, upper, hidden = forward(inputs, current[0], current[1])
        result = jnp.dot(hidden, current[2], preferred_element_type=jnp.float32)
        output_list.append((result * mask[:, None]).astype(jnp.bfloat16))
        outer_cot = out_cotangent[0, index] * mask[:, None].astype(jnp.bfloat16)
        partial_grads = backward(inputs, gate, upper, hidden, current[2], outer_cot)
        partial_grads = lax.psum(
            (partial_grads[0], partial_grads[1], partial_grads[2]), ("tok", "seq")
        )
        totals = tuple((held + grad for held, grad in zip(totals, partial_grads)))
    levels = jnp.stack(level_list)
    finals = own_units(totals, start, piece)
    fast_out = jnp.stack(output_list)[None]
    return (fast_out, finals[0], finals[1], finals[2], levels)


def solution(mesh):
    placed = (
        P("seq", None, "tok", None),
        P("seq", None, "tok", None),
        P("seq", None, "tok", None),
        P("seq", None, "tok"),
        P("seq", None),
        P(),
        P(),
        P(),
        P(),
        P("seq", None, "tok", None),
    )
    return jax.shard_map(
        per_device,
        mesh=mesh,
        in_specs=placed,
        out_specs=(
            P("seq", None, "tok", None),
            P(None, "tok"),
            P(None, "tok"),
            P("tok", None),
            P(None, "tok"),
        ),
        check_vma=False,
    )
```

profile of v0, /device:TPU:0, one launch (start us, length us, event | category | flops | bytes accessed | tf_op | source)
XLA Modules:
  0.0 418.5 jit_solution(18340729871907005278)
XLA Ops:
  8.0 1.3 fusion.117
  10.0 3.4 fusion.59
  13.4 2.0 fusion.61
  16.3 2.0 fusion.96
  18.3 1.3 copy-done.25
  19.6 3.9 convolution_bitcast_fusion.3
  23.6 4.0 convolution_bitcast_fusion.2
  27.6 4.5 %fusion.69 = f32[512,512]{1,0:T(8,128)} fusion(f32[1024,512]{1,0:T(8,128)} %fusion.61, f32[1024,512]{1,0:T(8,128)} %fusion.59, bf16[1,2,1024,512]{3,2,1,0:T(8,128)(2,1)} %param.11, f32[1024]{0:T(1024)S(1)} %divide_negate_fusion.1), kind=kOutput, calls=%fused_computation.101 | convolution fusion | flops 541589504 | bytes 6295552 | tf_op jit(solution)/shard_map/dot_general | solution.py:20
  32.2 1.3 copy.15
  34.9 1.3 copy.17
  39.9 13.6 %reduce-scatter.7.cloned.1.call-done = f32[512,128]{0,1:T(8,128)} async-done(((f32[512,512]{0,1:T(8,128)}), f32[512,128]{0,1:T(8,128)}) %reduce-scatter.7.cloned.1.call-update) | async-done | bytes 262160 | tf_op jit(solution)/shard_map/reduce_scatter | solution.py:83
  55.9 25.9 %reduce-scatter.9.cloned.1.call-done = f32[512,128]{0,1:T(8,128)} async-done(((f32[512,512]{0,1:T(8,128)}), f32[512,128]{0,1:T(8,128)}) %reduce-scatter.9.cloned.1.call-update) | async-done | bytes 262160 | tf_op jit(solution)/shard_map/reduce_scatter | solution.py:84
  82.9 19.3 %all_gather.18 = bf16[512,512]{0,1:T(8,128)(2,1)S(1)} all-gather(bf16[512,128]{0,1:T(8,128)(2,1)S(1)} %multiply_convert_fusion.13), channel_id=1, replica_groups=mesh['tok'=4,'seq'=8] {'tok'}, dimensions={1}, use_global_device_ids=true | all-gather | bytes 655360 | tf_op jit(solution)/shard_map/all_gather | solution.py:96
  103.4 20.1 %all_gather.19 = bf16[512,512]{0,1:T(8,128)(2,1)S(1)} all-gather(bf16[512,128]{0,1:T(8,128)(2,1)S(1)} %multiply_convert_fusion.12), channel_id=1, replica_groups=mesh['tok'=4,'seq'=8] {'tok'}, dimensions={1}, use_global_device_ids=true | all-gather | bytes 655360 | tf_op jit(solution)/shard_map/all_gather | solution.py:97
  125.7 1.3 copy-done.17
  127.0 2.1 fusion.70
  130.7 1.3 multiply_reduce_fusion.6
  132.1 2.0 fusion.55
  134.2 2.2 fusion.23
  137.4 1.8 fusion.72
  139.2 16.7 %reduce-scatter.17.cloned.1.call-done = f32[128,512]{1,0:T(8,128)} async-done(((f32[512,512]{1,0:T(8,128)}), f32[128,512]{1,0:T(8,128)}) %reduce-scatter.17.cloned.1.call-update) | async-done | bytes 262160 | tf_op jit(solution)/shard_map/reduce_scatter | solution.py:85
  155.9 1.2 multiply_reduce_fusion.3
  157.1 16.4 %all_gather.20 = bf16[512,512]{1,0:T(8,128)(2,1)S(1)} all-gather(bf16[128,512]{1,0:T(8,128)(2,1)S(1)} %get-tuple-element.23), channel_id=1, replica_groups=mesh['tok'=4,'seq'=8] {'tok'}, dimensions={0}, use_global_device_ids=true | all-gather | bytes 655360 | tf_op jit(solution)/shard_map/all_gather | solution.py:98
  173.5 2.0 fusion.99
  175.5 1.4 copy-done.23
  176.8 2.3 convolution_bitcast_fusion.1
  179.4 18.9 %all_gather.23 = bf16[512,512]{1,0:T(8,128)(2,1)S(1)} all-gather(bf16[128,512]{1,0:T(8,128)(2,1)S(1)} %multiply_convert_fusion.8), channel_id=1, replica_groups=mesh['tok'=4,'seq'=8] {'tok'}, dimensions={0}, use_global_device_ids=true | all-gather | bytes 655360 | tf_op jit(solution)/shard_map/all_gather | solution.py:98
  198.3 3.3 fusion.73
  201.7 1.8 convolution_bitcast_fusion
  203.5 4.5 %fusion.49 = f32[512,512]{1,0:T(8,128)} fusion(f32[1024,512]{1,0:T(8,128)} %fusion.73, f32[512,1024]{0,1:T(8,128)} %copy-done.16, bf16[1,2,1024,512]{3,2,1,0:T(8,128)(2,1)} %param.12), kind=kOutput, calls=%fused_computation.84 | convolution fusion | flops 540016640 | bytes 6291456 | tf_op jit(solution)/shard_map/dot_general | solution.py:28
  208.1 2.1 fusion.74
  210.2 5.2 %fusion.51 = f32[512,512]{1,0:T(8,128)} fusion(f32[1024,512]{1,0:T(8,128)} %fusion.73, f32[512,1024]{0,1:T(8,128)} %get-tuple-element.32, f32[512,1024]{0,1:T(8,128)} %copy-done.16, bf16[1,2,1024,512]{3,2,1,0:T(8,128)(2,1)S(1)} %copy-done.5), kind=kOutput, calls=%fused_computation.86 | convolution fusion | flops 542113792 | bytes 8388608 | tf_op jit(solution)/shard_map/dot_general | solution.py:27
  215.4 1.4 multiply_reduce_fusion.5
  217.0 19.8 %all_gather.21 = bf16[512,512]{0,1:T(8,128)(2,1)S(1)} all-gather(bf16[512,128]{0,1:T(8,128)(2,1)S(1)} %multiply_convert_fusion.10), channel_id=1, replica_groups=mesh['tok'=4,'seq'=8] {'tok'}, dimensions={1}, use_global_device_ids=true | all-gather | bytes 655360 | tf_op jit(solution)/shard_map/all_gather | solution.py:96
  236.7 2.1 fusion.41
  238.8 3.8 reduce-scatter.15.cloned.1.call-done
  242.6 1.4 multiply_reduce_fusion.4
  244.1 15.2 %all_gather.22 = bf16[512,512]{0,1:T(8,128)(2,1)S(1)} all-gather(bf16[512,128]{0,1:T(8,128)(2,1)S(1)} %multiply_convert_fusion.9), channel_id=1, replica_groups=mesh['tok'=4,'seq'=8] {'tok'}, dimensions={1}, use_global_device_ids=true | all-gather | bytes 655360 | tf_op jit(solution)/shard_map/all_gather | solution.py:97
  259.3 2.3 fusion.2
  262.1 1.8 fusion.35
  263.9 2.4 fusion.36
  266.3 1.8 convolution_add_fusion
  269.4 1.9 fusion.33
  271.4 12.0 %all-reduce.1 = (f32[1,128]{1,0:T(1,128)S(1)}, f32[1,128]{1,0:T(1,128)S(1)}) all-reduce(f32[1,128]{1,0:T(1,128)S(1)} %bitcast.237, f32[1,128]{1,0:T(1,128)S(1)} %bitcast.238), channel_id=1, replica_groups=mesh['tok'=4,'seq'=8] {'seq'}, use_global_device_ids=true, to_apply=%region_24.25 | all-reduce | flops 256 | bytes 2048 | tf_op jit(solution)/shard_map/pmax | solution.py:88
  283.9 1.9 fusion.34
  285.9 1.5 maximum_bitcast_fusion
  287.4 119.9 %all-reduce.4.cloned.1.call-done = (f32[512,512]{0,1:T(8,128)}, f32[512,512]{0,1:T(8,128)}, f32[512,512]{1,0:T(8,128)}) async-done(((f32[512,512]{0,1:T(8,128)}, f32[512,512]{0,1:T(8,128)}, f32[512,512]{1,0:T(8,128)}), (f32[512,512]{0,1:T(8,128)}, f32[512,512]{0,1:T(8,128)}, f32[512,512]{1,0:T(8,128)})) %all-reduce.4.cloned.1.call-update) | async-done | bytes 3145744 | tf_op jit(solution)/shard_map/psum | solution.py:106
  410.0 1.7 constant_dynamic-slice_fusion
  (116 shorter events, 20.8 us)
Async XLA Ops:
  7.2 6.2 %copy-start = (bf16[1,2,1024,512]{3,2,1,0:T(8,128)(2,1)S(1)}, bf16[1,2,1024,512]{3,2,1,0:T(8,128)(2,1)}, u32[]{:S(2)}) copy-start(bf16[1,2,1024,512]{3,2,1,0:T(8,128)(2,1)} %param.10) | copy-start | bytes 6291460
  7.2 6.2 %copy-start.21 = (bf16[512,512]{1,0:T(8,128)(2,1)S(1)}, bf16[512,512]{1,0:T(8,128)(2,1)}, u32[]{:S(2)}) copy-start(bf16[512,512]{1,0:T(8,128)(2,1)} %param.17) | copy-start | bytes 1572868
  7.2 46.3 %reduce-scatter.7.cloned.1.call-start = ((), (), s32[]{:S(2)}) async-start(), calls=%async_computation.6 | async-start | bytes 1310720 | tf_op jit(solution)/shard_map/reduce_scatter | solution.py:83
  13.4 2.1 copy-start.28
  13.4 2.9 copy-start.1
  15.5 4.1 copy-start.19
  18.3 1.3 copy-start.25
  23.5 58.2 %reduce-scatter.9.cloned.1.call-start = ((), (), s32[]{:S(2)}) async-start(), calls=%async_computation.7 | async-start | bytes 1310720 | tf_op jit(solution)/shard_map/reduce_scatter | solution.py:84
  27.6 103.1 %reduce-scatter.11.cloned.1.call-start = ((), (), s32[]{:S(2)}) async-start(), calls=%async_computation.8 | async-start | bytes 1310720 | tf_op jit(solution)/shard_map/reduce_scatter | solution.py:85
  32.2 123.7 %reduce-scatter.17.cloned.1.call-start = ((), (), s32[]{:S(2)}) async-start(), calls=%async_computation.11 | async-start | bytes 1310720 | tf_op jit(solution)/shard_map/reduce_scatter | solution.py:85
  123.5 0.8 copy-start.11
  124.4 1.3 copy-start.13
  124.4 2.6 copy-start.26
  125.7 1.3 copy-start.17
  129.1 86.3 %reduce-scatter.13.cloned.1.call-start = ((), (), s32[]{:S(2)}) async-start(), calls=%async_computation.9 | async-start | bytes 1310720 | tf_op jit(solution)/shard_map/reduce_scatter | solution.py:83
  130.7 3.4 copy-start.4
  130.7 3.4 copy-start.12
  134.1 2.3 copy-start.16
  134.1 3.3 copy-start.8
  136.4 1.0 copy-start.29
  137.4 18.5 %copy-start.27 = (f32[128,512]{1,0:T(8,128)S(1)}, f32[128,512]{1,0:T(8,128)}, u32[]{:S(2)}) copy-start(f32[128,512]{1,0:T(8,128)} %reduce-scatter.11.cloned.1.call-done) | copy-start | bytes 786436
  157.1 19.7 %copy-start.14 = (f32[512,1024]{0,1:T(8,128)S(1)}, f32[512,1024]{0,1:T(8,128)}, u32[]{:S(2)}) copy-start(f32[512,1024]{0,1:T(8,128)} %copy-done.13) | copy-start | bytes 6291460
  157.1 19.7 %copy-start.18 = (f32[512,1024]{0,1:T(8,128)S(1)}, f32[512,1024]{0,1:T(8,128)}, u32[]{:S(2)}) copy-start(f32[512,1024]{0,1:T(8,128)} %copy-done.17) | copy-start | bytes 6291460
  175.5 1.4 copy-start.23
  179.2 63.4 %reduce-scatter.15.cloned.1.call-start = ((), (), s32[]{:S(2)}) async-start(), calls=%async_computation.10 | async-start | bytes 1310720 | tf_op jit(solution)/shard_map/reduce_scatter | solution.py:84
  179.4 22.3 %copy-start.15 = (f32[512,1024]{0,1:T(8,128)S(1)}, f32[512,1024]{0,1:T(8,128)}, u32[]{:S(2)}) copy-start(f32[512,1024]{0,1:T(8,128)} %copy-done.13) | copy-start | bytes 6291460
  179.4 22.3 %copy-start.24 = (f32[1024,512]{1,0:T(8,128)S(1)}, f32[1024,512]{1,0:T(8,128)}, u32[]{:S(2)}) copy-start(f32[1024,512]{1,0:T(8,128)} %copy-done.23) | copy-start | bytes 6291460
  203.5 4.6 %copy-start.9 = (bf16[1,2,1024,512]{3,2,1,0:T(8,128)(2,1)S(1)}, bf16[1,2,1024,512]{3,2,1,0:T(8,128)(2,1)}, u32[]{:S(2)}) copy-start(bf16[1,2,1024,512]{3,2,1,0:T(8,128)(2,1)} %param.19) | copy-start | bytes 6291460
  208.0 199.2 %all-reduce.4.cloned.1.call-start = ((), (), s32[]{:S(2)}) async-start(), calls=%async_computation.12 | async-start | bytes 6291456 | tf_op jit(solution)/shard_map/psum | solution.py:106
  208.1 2.1 copy-start.5
  210.2 5.2 %copy-start.3 = (f32[512,128]{0,1:T(8,128)S(1)}, f32[512,128]{0,1:T(8,128)}, u32[]{:S(2)}) copy-start(f32[512,128]{0,1:T(8,128)} %reduce-scatter.7.cloned.1.call-done) | copy-start | bytes 786436
  215.4 21.4 %copy-start.6 = (bf16[1,2,1024,512]{3,2,1,0:T(8,128)(2,1)S(1)}, bf16[1,2,1024,512]{3,2,1,0:T(8,128)(2,1)}, u32[]{:S(2)}) copy-start(bf16[1,2,1024,512]{3,2,1,0:T(8,128)(2,1)} %param.12) | copy-start | bytes 6291460
  217.0 25.6 %copy-start.2 = (f32[512,128]{0,1:T(8,128)S(1)}, f32[512,128]{0,1:T(8,128)}, u32[]{:S(2)}) copy-start(f32[512,128]{0,1:T(8,128)} %reduce-scatter.9.cloned.1.call-done) | copy-start | bytes 786436
  242.6 16.8 %copy-start.20 = (f32[512,1024]{0,1:T(8,128)S(1)}, f32[512,1024]{0,1:T(8,128)}, u32[]{:S(2)}) copy-start(f32[512,1024]{0,1:T(8,128)} %fusion.41) | copy-start | bytes 6291460
  259.3 2.4 copy-start.7
  259.3 2.5 copy-start.22
  259.3 2.8 copy-start.33
  262.1 4.2 copy-start.30
  262.1 1.8 copy-start.32
  263.9 2.4 copy-start.10
  263.9 2.4 copy-start.31
Sparse Core Ops, SparseCore 0:
  23.6 29.8 reduce-scatter.6
  55.9 25.8 reduce-scatter.8
  84.1 34.8 reduce-scatter.10
  129.3 26.5 reduce-scatter.16
  179.3 29.0 reduce-scatter.12
  210.6 31.9 reduce-scatter.14
  268.2 138.9 all-reduce.3
where the time goes:
time: 419 us
  waiting for transfers between devices  180 us (43%)
  blocking collectives  122 us (29%)
  matrix products  64.8 us (15%)
  other arithmetic  20.7 us (5%)
  between operations  16.6 us (4%)
  local copies, waits for them, and re-layouts  14.5 us (3%)
    psum x1, waiting for transfers between devices, per_device(): lax.psum((partial_grads[0], partial_grads[1], partial_grads[2]), ('tok',...  120 us
    all_gather x2, blocking collectives, per_device(): lax.all_gather(rounded[0], 'tok', axis=1, tiled=True)  39.1 us
    all_gather x2, blocking collectives, per_device(): lax.all_gather(rounded[2], 'tok', axis=0, tiled=True)  35.3 us
    all_gather x2, blocking collectives, per_device(): lax.all_gather(rounded[1], 'tok', axis=1, tiled=True)  35.3 us
    reduce_scatter x2, waiting for transfers between devices, per_device(): lax.psum_scatter(grads[1], 'tok', scatter_dimension=1, tiled=True)  29.6 us
    reduce_scatter x2, waiting for transfers between devices, per_device(): lax.psum_scatter(grads[2], 'tok', scatter_dimension=0, tiled=True)  16.7 us
    dot_general x4, matrix products, backward(): lax.dot_general(inputs, d_gate, first, preferred_element_type=jnp.float32)  13.8 us
    reduce_scatter x2, waiting for transfers between devices, per_device(): lax.psum_scatter(grads[0], 'tok', scatter_dimension=1, tiled=True)  13.6 us
  transfers between devices with their start and end apart: 7, of which 5 were waited for; matrix products, arithmetic and copies ran while one was open for 14% of the time, Pallas kernels for 0%

commit v1 on v0

v1 whole, which is shorter than its diff:
```python
import functools

import jax
import jax.numpy as jnp
from jax import lax
from jax.experimental import pallas as pl
from jax.experimental.pallas import tpu as pltpu
from jax.sharding import PartitionSpec as P

momentum_keep = 0.9
step_rate = 3.0
tiny_value = 1e-06
MESH = pl.DeviceIdType.MESH
f32 = jnp.float32
bf16 = jnp.bfloat16


def dot_nt(a, b):
    return lax.dot_general(a, b, (((1,), (1,)), ((), ())), preferred_element_type=f32)


def dot_nn(a, b):
    return lax.dot_general(a, b, (((1,), (0,)), ((), ())), preferred_element_type=f32)


def dot_tn(a, b):
    return lax.dot_general(a, b, (((0,), (0,)), ((), ())), preferred_element_type=f32)


def plan_stages(nseq, piece, width):
    stages = []
    q, w, bit = piece, width, 1
    while bit < nseq:
        if w > 128:
            w //= 2
            stages.append((bit, "lane", q, w))
        else:
            q //= 2
            stages.append((bit, "unit", q, w))
        bit *= 2
    return stages, q, w


def kernel(
    n, nseq, chunks, unit, stages,
    scale_ref, keys, values, queries, cots, w_init, rows_ref,
    out_hbm, grad_ref, level_ref,
    kv, vv, qv, cv, w, sbuf, rbuf, state, mom, acc, tot, hid, fo, lev, levr, zs, zr, gat, *rest,
):
    ns = len(stages)
    sb, rb = rest[:ns], rest[ns:2 * ns]
    in_sem, s_send, s_recv, w_send, w_recv, o_sem, f_send, f_recv, l_send, l_recv, g_send, g_recv, z_send, z_recv, y_send, y_recv = rest[2 * ns:]
    dim = kv.shape[2]
    tokens = kv.shape[1]
    piece = chunks * unit // n
    me = lax.axis_index("tok")
    seq = lax.axis_index("seq")
    half = n // 2
    low = me < half
    inn = jnp.where(low, me + 1, me - 1)
    mid = jnp.logical_or(me == half - 1, me == half)
    has_out = jnp.logical_and(me > 0, me < n - 1)
    out = jnp.where(low, jnp.maximum(me - 1, 0), jnp.minimum(me + 1, n - 1))
    kind = jnp.where(mid, 1, 0)

    first_in = [
        pltpu.make_async_copy(keys.at[0], kv.at[0], in_sem.at[0]),
        pltpu.make_async_copy(w_init, w.at[pl.ds(0, chunks)], in_sem.at[1]),
        pltpu.make_async_copy(values.at[0], vv.at[0], in_sem.at[2]),
    ]
    later_in = [
        pltpu.make_async_copy(keys.at[1], kv.at[1], in_sem.at[3]),
        pltpu.make_async_copy(values.at[1], vv.at[1], in_sem.at[4]),
        pltpu.make_async_copy(queries, qv, in_sem.at[5]),
        pltpu.make_async_copy(cots, cv, in_sem.at[6]),
    ]
    for copy in first_in + later_in:
        copy.start()

    barrier = pltpu.get_barrier_semaphore()
    for d in range(1, n):
        pl.semaphore_signal(barrier, inc=1, device_id={"tok": lax.rem(me + d, n)}, device_id_type=MESH)
    partners = []
    for bit, _, _, _ in stages:
        side = lax.rem(seq // bit, 2)
        partner = seq + bit * (1 - 2 * side)
        partners.append((side, partner))
        pl.semaphore_signal(barrier, inc=1, device_id={"seq": partner}, device_id_type=MESH)
    pl.semaphore_wait(barrier, n - 1 + ns)

    lev[...] = jnp.zeros_like(lev)
    for copy in first_in:
        copy.wait()
    scale = scale_ref[0]

    @pl.when(mid)
    def _():
        def fill(c, carry):
            state[c] = w[c].astype(f32)
            mom[c] = jnp.zeros(mom.shape[1:], f32)
            return carry
        lax.fori_loop(0, chunks, fill, 0)

    def send_copy(t):
        return pltpu.make_async_remote_copy(
            src_ref=sbuf.at[t], dst_ref=rbuf.at[kind, t], send_sem=s_send.at[t],
            recv_sem=s_recv.at[kind, t], device_id={"tok": inn}, device_id_type=MESH)

    def recv_copy(k, t):
        return pltpu.make_async_remote_copy(
            src_ref=sbuf.at[t], dst_ref=rbuf.at[k, t], send_sem=s_send.at[t],
            recv_sem=s_recv.at[k, t], device_id={"tok": inn}, device_id_type=MESH)

    def weight_copy(t):
        return pltpu.make_async_remote_copy(
            src_ref=w.at[t + chunks], dst_ref=w.at[t + chunks], send_sem=w_send.at[t],
            recv_sem=w_recv.at[t], device_id={"tok": out}, device_id_type=MESH)

    def parts(wt, x, e, row):
        ab = dot_nt(w[wt, 0:2].reshape(2 * unit, dim), x)
        r = dot_nt(w[wt, 2], e) * row
        a, b = ab[:unit], ab[unit:]
        s = jax.nn.sigmoid(a)
        g = a * s
        h = (g * b * row).astype(bf16)
        eb = (r * g).astype(bf16)
        ea = (r * b * s * (1.0 + a * (1.0 - s))).astype(bf16)
        gg = dot_nn(jnp.concatenate([ea, eb], axis=0), x)
        gw = dot_nn(h, e)
        return h, gg, gw

    def finish(t):
        c = lax.rem(t, chunks)
        recv_copy(1, t).wait_recv()
        s = sbuf[t].astype(f32) + rbuf[1, t].astype(f32)
        top = jnp.abs(s[0])
        top = functools.reduce(jnp.maximum, [top[:, k:k + 128] for k in range(0, dim, 128)])
        lev[t] = jnp.max(top.T, axis=0, keepdims=True)
        m = momentum_keep * mom[c] + s * (1.0 / scale)
        mom[c] = m
        first = w[c].astype(f32)
        ref_norm = jnp.sqrt(jnp.sum(first * first, axis=2, keepdims=True) + tiny_value)
        st = state[c] - step_rate * m
        st = st * (ref_norm / jnp.sqrt(jnp.sum(st * st, axis=2, keepdims=True) + tiny_value))
        state[c] = st
        w[t + chunks] = st.astype(bf16)

        @pl.when(has_out)
        def _():
            weight_copy(t).start()

    def arrive(t):
        @pl.when(jnp.logical_not(mid))
        def _():
            weight_copy(t).wait_recv()

            @pl.when(has_out)
            def _():
                weight_copy(t).start()

    def outer(block, c, first):
        h, gg, gw = parts((block + 1) * chunks + c, qv[block], cv[block], rows_ref[block, 1:2])
        units = pl.ds(pl.multiple_of(c * unit, unit), unit)
        hid[units, :] = h
        for k, g in enumerate((gg[:unit], gg[unit:], gw)):
            tot[k, units, :] = g if first else tot[k, units, :] + g

    def write_out(block):
        tile = min(256, tokens)
        down = w[pl.ds((block + 1) * chunks, chunks), 2].reshape(chunks * unit, dim)
        for start in range(0, tokens, tile):
            fo[block, start:start + tile] = dot_tn(hid[:, start:start + tile], down).astype(bf16)
        pltpu.make_async_copy(fo.at[block], out_hbm.at[block], o_sem.at[block]).start()

    def step(t, carry):
        block = t // chunks
        c = lax.rem(t, chunks)

        @pl.when(t == chunks - 1)
        def _():
            for copy in later_in:
                copy.wait()

        @pl.when(t >= chunks)
        def _():
            arrive(t - chunks)
        h, gg, gw = parts(t, kv[block], vv[block], rows_ref[block, 0:1])
        acc[0:2] = gg.reshape(2, unit, dim)
        acc[2] = gw

        @pl.when(has_out)
        def _():
            recv_copy(0, t).wait_recv()
            acc[...] += rbuf[0, t].astype(f32)
        sbuf[t] = acc[...].astype(bf16)
        send_copy(t).start()

        @pl.when(jnp.logical_and(mid, t > 0))
        def _():
            finish(t - 1)

        @pl.when(t >= chunks)
        def _():
            outer(0, c, True)
        return carry

    lax.fori_loop(0, 2 * chunks, step, 0)

    @pl.when(mid)
    def _():
        finish(2 * chunks - 1)
    write_out(0)

    def last(c, carry):
        arrive(chunks + c)
        outer(1, c, False)
        return carry
    lax.fori_loop(0, chunks, last, 0)

    qo, lo = 0, 0
    q, wd = piece, dim
    places = []
    for k, (bit, how, q2, w2) in enumerate(stages):
        side, partner = partners[k]
        if how == "lane":
            keep_q, give_q = qo, qo
            keep_l, give_l = lo + side * w2, lo + (1 - side) * w2
        else:
            keep_q, give_q = qo + side * q2, qo + (1 - side) * q2
            keep_l, give_l = lo, lo

        def region(p, uo, ln, q2=q2, w2=w2):
            return (slice(None), pl.ds(pl.multiple_of(p * piece + uo, 16), q2), pl.ds(pl.multiple_of(ln, 128), w2))
        for p in range(n):
            sb[k][:, p] = tot[region(p, give_q, give_l)].astype(bf16)
        copy = pltpu.make_async_remote_copy(
            src_ref=sb[k], dst_ref=rb[k], send_sem=f_send.at[k], recv_sem=f_recv.at[k],
            device_id={"seq": partner}, device_id_type=MESH)
        lcopy = pltpu.make_async_remote_copy(
            src_ref=lev, dst_ref=levr.at[k], send_sem=l_send.at[k], recv_sem=l_recv.at[k],
            device_id={"seq": partner}, device_id_type=MESH)
        copy.start()
        lcopy.start()
        if k == 0:
            write_out(1)
        lcopy.wait()
        lev[...] = jnp.maximum(lev[...], levr[k])
        copy.wait()
        for p in range(n):
            where = region(p, keep_q, keep_l)
            tot[where] = tot[where] + rb[k][:, p].astype(f32)
        qo, lo, q, wd = keep_q, keep_l, q2, w2
        places.append((qo, lo, q, wd))

    for p in range(n):
        zs[p] = tot[:, pl.ds(pl.multiple_of(p * piece + qo, 16), q), pl.ds(pl.multiple_of(lo, 128), wd)].astype(bf16)
    spread = []
    for d in range(1, n):
        p = lax.rem(me + d, n)
        spread.append(pltpu.make_async_remote_copy(
            src_ref=zs.at[p], dst_ref=zr.at[d - 1], send_sem=z_send.at[d - 1], recv_sem=z_recv.at[d - 1],
            device_id={"tok": p}, device_id_type=MESH))
        spread.append(pltpu.make_async_remote_copy(
            src_ref=lev, dst_ref=levr.at[ns + d - 1], send_sem=y_send.at[d - 1], recv_sem=y_recv.at[d - 1],
            device_id={"tok": p}, device_id_type=MESH))
    for copy in spread:
        copy.start()
    total = tot[:, pl.ds(pl.multiple_of(me * piece + qo, 16), q), pl.ds(pl.multiple_of(lo, 128), wd)]
    for copy in spread:
        copy.wait()
    top = lev[...]
    for d in range(1, n):
        total = total + zr[d - 1].astype(f32)
        top = jnp.maximum(top, levr[ns + d - 1])
    level_ref[...] = top
    gat[:, pl.ds(pl.multiple_of(qo, 16), q), pl.ds(pl.multiple_of(lo, 128), wd)] = total.astype(bf16)
    for k in range(ns - 1, -1, -1):
        uo, ln, q2, w2 = places[k]
        mine = gat.at[:, pl.ds(pl.multiple_of(uo, 16), q2), pl.ds(pl.multiple_of(ln, 128), w2)]
        copy = pltpu.make_async_remote_copy(
            src_ref=mine, dst_ref=mine, send_sem=g_send.at[k], recv_sem=g_recv.at[k],
            device_id={"seq": partners[k][1]}, device_id_type=MESH)
        copy.start()
        copy.wait()
    grad_ref[...] = gat[...].astype(f32)

    def drain(t, carry):
        send_copy(t).wait_send()

        @pl.when(has_out)
        def _():
            weight_copy(t).wait_send()
        return carry
    lax.fori_loop(0, 2 * chunks, drain, 0)
    for block in range(2):
        pltpu.make_async_copy(fo.at[block], out_hbm.at[block], o_sem.at[block]).wait()


def per_device(
    keys, values, queries, token_rate, valid_count, loss_scale, w_gate, w_up, w_down, out_cotangent
):
    rows = keys.shape[2]
    blocks = keys.shape[1]
    dim = keys.shape[3]
    width = w_gate.shape[1]
    n = lax.axis_size("tok")
    nseq = lax.axis_size("seq")
    where = lax.axis_index("tok")
    piece = width // n
    unit = min(64, piece)
    chunks = width // unit
    stages, q, wd = plan_stages(nseq, piece, dim)
    ns = len(stages)
    positions = where * rows + jnp.arange(rows, dtype=jnp.int32)
    count = valid_count[0][:, None]
    mask = (positions[None] < count).astype(f32)
    factor = -(loss_scale[0] * token_rate[0] * mask / count.astype(f32))
    lanes = jnp.stack([factor, mask], axis=1)
    weights = jnp.stack([w_gate.T, w_up.T, w_down])
    weights = weights.reshape(3, chunks, unit, dim).transpose(1, 0, 2, 3)
    any_spec = pl.BlockSpec(memory_space=pl.ANY)
    vmem = pl.BlockSpec(memory_space=pltpu.VMEM)
    dma = pltpu.SemaphoreType.DMA
    scratch = [
        pltpu.VMEM((blocks, rows, dim), bf16), pltpu.VMEM((blocks, rows, dim), bf16),
        pltpu.VMEM((blocks, rows, dim), bf16), pltpu.VMEM((blocks, rows, dim), bf16),
        pltpu.VMEM((3 * chunks, 3, unit, dim), bf16),
        pltpu.VMEM((2 * chunks, 3, unit, dim), bf16),
        pltpu.VMEM((2, 2 * chunks, 3, unit, dim), bf16),
        pltpu.VMEM((chunks, 3, unit, dim), f32), pltpu.VMEM((chunks, 3, unit, dim), f32),
        pltpu.VMEM((3, unit, dim), f32),
        pltpu.VMEM((3, width, dim), f32),
        pltpu.VMEM((width, rows), bf16),
        pltpu.VMEM((blocks, rows, dim), bf16),
        pltpu.VMEM((2 * chunks, 1, unit), f32),
        pltpu.VMEM((ns + n - 1, 2 * chunks, 1, unit), f32),
        pltpu.VMEM((n, 3, q, wd), bf16), pltpu.VMEM((n - 1, 3, q, wd), bf16),
        pltpu.VMEM((3, piece, dim), bf16),
    ]
    scratch += [pltpu.VMEM((3, n, a, b), bf16) for _, _, a, b in stages] * 2
    scratch += [
        dma((7,)), dma((2 * chunks,)), dma((2, 2 * chunks)), dma((2 * chunks,)), dma((2 * chunks,)),
        dma((2,)), dma((ns,)), dma((ns,)), dma((ns,)), dma((ns,)), dma((ns,)), dma((ns,)),
        dma((n - 1,)), dma((n - 1,)), dma((n - 1,)), dma((n - 1,)),
    ]
    fast_out, grads, levels = pl.pallas_call(
        functools.partial(kernel, n, nseq, chunks, unit, stages),
        out_shape=(
            jax.ShapeDtypeStruct((blocks, rows, dim), bf16),
            jax.ShapeDtypeStruct((3, piece, dim), f32),
            jax.ShapeDtypeStruct((2 * chunks, 1, unit), f32),
        ),
        in_specs=[pl.BlockSpec(memory_space=pltpu.SMEM)] + [any_spec] * 5 + [vmem],
        out_specs=(any_spec, vmem, vmem),
        scratch_shapes=scratch,
        compiler_params=pltpu.CompilerParams(
            collective_id=0, has_side_effects=True, vmem_limit_bytes=60 * 2**20
        ),
    )(loss_scale, keys[0], values[0], queries[0], out_cotangent[0], weights, lanes)
    levels = lax.dynamic_slice_in_dim(levels.reshape(blocks, width), where * piece, piece, 1)
    return (fast_out[None], grads[0].T, grads[1].T, grads[2], levels)


def solution(mesh):
    placed = (
        P("seq", None, "tok", None),
        P("seq", None, "tok", None),
        P("seq", None, "tok", None),
        P("seq", None, "tok"),
        P("seq", None),
        P(),
        P(),
        P(),
        P(),
        P("seq", None, "tok", None),
    )
    return jax.shard_map(
        per_device,
        mesh=mesh,
        in_specs=placed,
        out_specs=(
            P("seq", None, "tok", None),
            P(None, "tok"),
            P(None, "tok"),
            P("tok", None),
            P(None, "tok"),
        ),
        check_vma=False,
    )
```

time: 419 us -> 142 us (0.34)
  waiting for transfers between devices: 180 us -> 0 us
  Pallas kernels: 0 us -> 126 us
  blocking collectives: 122 us -> 0 us
  matrix products: 64.8 us -> 0 us
  between operations: 16.6 us -> 1.4 us
  other arithmetic: 20.7 us -> 6.24 us
  local copies, waits for them, and re-layouts: 14.5 us -> 8.52 us
    pallas_call x0 -> x1, Pallas kernels: none -> 126 us  [per_device(): pl.pallas_call(functools.partial(kernel, n, nseq, chunks, unit, stages),...]
    psum x1 -> x0, waiting for transfers between devices: 120 us -> none  [per_device(): lax.psum((partial_grads[0], partial_grads[1], partial_grads[2]), ('tok',...]
    all_gather x6 -> x0, blocking collectives: 110 us -> none  [the longest x2 39.1 us: per_device(): lax.all_gather(rounded[0], 'tok', axis=1, tiled=True)]
    dot_general x26 -> x0, matrix products: 64.8 us -> none  [the longest x4 13.8 us: backward(): lax.dot_general(inputs, d_gate, first, preferred_element_type=jnp.float32)]
    reduce_scatter x6 -> x0, waiting for transfers between devices: 60 us -> none  [the longest x2 29.6 us: per_device(): lax.psum_scatter(grads[1], 'tok', scatter_dimension=1, tiled=True)]
    pmax x1 -> x0, blocking collectives: 12 us -> none  [per_device(): level_list.append(lax.pmax(level_piece, 'seq'))]
    unnamed x72 -> x7, local copies, waits for them, and re-layouts: 10.4 us -> 3 us
    convert_element_type x12 -> x2, other arithmetic: 8.56 us -> 1.39 us  [the longest x1 0.73 us: per_device(): mask = (positions[None] < count).astype(f32)]
  transfers between devices with their start and end apart: 7 -> 0, of which waited for: 5 -> 0; matrix products, arithmetic and copies ran while one was open for 14% -> 0% of each run, Pallas kernels for 0% -> 0%
where the time goes in v1:
time: 142 us
  Pallas kernels  126 us (89%)
  local copies, waits for them, and re-layouts  8.52 us (6%)
  other arithmetic  6.24 us (4%)
    pallas_call x1, Pallas kernels, per_device(): pl.pallas_call(functools.partial(kernel, n, nseq, chunks, unit, stages),...  126 us
    unnamed x7, local copies, waits for them, and re-layouts  3 us

profile of v1, /device:TPU:0, one launch (start us, length us, event | category | flops | bytes accessed | tf_op | source)
XLA Modules:
  0.0 141.7 jit_solution(6128648555249580322)
XLA Ops:
  0.6 0.0 copy-start.1
  1.4 0.7 broadcast_multiply_fusion
  2.1 0.7 bitcast_convert_fusion
  2.7 0.7 fusion.1
  3.5 0.7 compare_convert_fusion
  4.2 0.6 pad_maximum_fusion.rows_ref
  4.8 1.3 copy.15
  6.1 1.3 copy.16
  7.3 0.0 copy-done.1
  7.3 1.3 maximum_bitcast_fusion.w_init
  8.7 125.5 %shard_map.137 = (bf16[2,1024,512]{2,1,0:T(8,128)(2,1)}, f32[3,128,512]{2,1,0:T(8,128)}, f32[16,1,64]{2,1,0:T(1,128)}) custom-call(f32[1]{0:T(128)} %copy.25.scale_ref, bf16[2,1024,512]{2,1,0:T(8,128)(2,1)} %bitcast.30, bf16[2,1024,512]{2,1,0:T(8,128)(2,1)} %bitcast.31, bf16[2,1024,512]{2,1,0:T(8,128)(2,1)} %bitcast.32, bf16[2,1024,512]{2,1,0:T(8,128)(2,1)} %bitcast.33, ...), custom_call_target="tpu_custom_call" | custom-call | tf_op jit(solution)/shard_map/pallas_call | solution.py:346
  134.2 0.0 copy-start
  134.2 0.5 broadcast.102
  134.7 1.5 %reduce.3 = f32[16,64]{1,0:T(8,128)S(1)} reduce(f32[16,1,64]{2,1,0:T(1,128)} %get-tuple-element.10, f32[]{:T(128)} %broadcast.102), dimensions={1}, to_apply=%get-tuple-element.10.reduce_sub_computation.3 | reduce | bytes 8196 | tf_op jit(solution)/shard_map/pallas_call | solution.py:346
  136.2 0.1 reshape.169
  136.3 0.6 constant_dynamic-slice_fusion
  136.8 1.9 %slice_bitcast_fusion = (f32[128,512]{1,0:T(8,128)}, f32[512,128]{0,1:T(8,128)S(1)}, f32[512,128]{0,1:T(8,128)S(1)}) fusion(f32[3,128,512]{2,1,0:T(8,128)} %get-tuple-element.9), kind=kLoop, calls=%fused_computation.1 | loop fusion | bytes 1572864 | tf_op jit(solution)/shard_map/squeeze | solution.py:361
  138.7 0.8 copy.18
  139.5 0.8 copy.19
  140.4 0.0 copy-done
  140.4 1.3 copy.26
  (1 shorter events, 0.0 us)
Async XLA Ops:
  0.6 6.7 %copy-start.1 = (bf16[512,512]{1,0:T(8,128)(2,1)S(1)}, bf16[512,512]{1,0:T(8,128)(2,1)}, u32[]{:S(2)}) copy-start(bf16[512,512]{1,0:T(8,128)(2,1)} %param.18) | copy-start | bytes 1572868
  134.2 6.2 %copy-start = (bf16[2,1024,512]{2,1,0:T(8,128)(2,1)S(1)}, bf16[2,1024,512]{2,1,0:T(8,128)(2,1)}, u32[]{:S(2)}) copy-start(bf16[2,1024,512]{2,1,0:T(8,128)(2,1)} %get-tuple-element.8) | copy-start | bytes 6291460

commit v2 on v1

--- a/solution.py
+++ b/solution.py
@@ -43,9 +43,9 @@
 
 def kernel(
     n, nseq, chunks, unit, stages,
-    scale_ref, keys, values, queries, cots, w_init, rows_ref,
-    out_hbm, grad_ref, level_ref,
-    kv, vv, qv, cv, w, sbuf, rbuf, state, mom, acc, tot, hid, fo, lev, levr, zs, zr, gat, *rest,
+    scale_ref, count_ref, keys, values, queries, cots, gate_in, up_in, down_in, rate_ref,
+    out_hbm, gate_out, up_out, down_out, level_ref,
+    kv, vv, qv, cv, wraw, rows_ref, w, sbuf, rbuf, state, mom, acc, tot, hid, fo, lev, levr, zs, zr, gat, *rest,
 ):
     ns = len(stages)
     sb, rb = rest[:ns], rest[ns:2 * ns]
@@ -65,7 +65,9 @@
 
     first_in = [
         pltpu.make_async_copy(keys.at[0], kv.at[0], in_sem.at[0]),
-        pltpu.make_async_copy(w_init, w.at[pl.ds(0, chunks)], in_sem.at[1]),
+        pltpu.make_async_copy(gate_in, wraw.at[0], in_sem.at[1]),
+        pltpu.make_async_copy(up_in, wraw.at[1], in_sem.at[7]),
+        pltpu.make_async_copy(down_in, wraw.at[2], in_sem.at[8]),
         pltpu.make_async_copy(values.at[0], vv.at[0], in_sem.at[2]),
     ]
     later_in = [
@@ -89,9 +91,25 @@
     pl.semaphore_wait(barrier, n - 1 + ns)
 
     lev[...] = jnp.zeros_like(lev)
-    for copy in first_in:
+    scale = scale_ref[0]
+    slots = lax.broadcasted_iota(jnp.int32, (1, tokens), 1) + me * tokens
+    for block in range(2):
+        count = count_ref[0, block]
+        mask = jnp.where(slots < count, 1.0, 0.0).astype(f32)
+        rows_ref[block, 1:2] = mask
+        rows_ref[block, 0:1] = -(scale * rate_ref[0, block:block + 1] * mask / count.astype(f32))
+    for copy in first_in[1:4]:
         copy.wait()
-    scale = scale_ref[0]
+    side_by = max(128, unit)
+    for k in range(2):
+        for start in range(0, chunks * unit, side_by):
+            turned = wraw[k, :, start:start + side_by].T
+            for off in range(0, side_by, unit):
+                w[(start + off) // unit, k] = turned[off:off + unit]
+    for c in range(chunks):
+        w[c, 2] = wraw[2, c * unit:(c + 1) * unit]
+    first_in[0].wait()
+    first_in[4].wait()
 
     @pl.when(mid)
     def _():
@@ -161,7 +179,7 @@
     def outer(block, c, first):
         h, gg, gw = parts((block + 1) * chunks + c, qv[block], cv[block], rows_ref[block, 1:2])
         units = pl.ds(pl.multiple_of(c * unit, unit), unit)
-        hid[units, :] = h
+        hid[block, units, :] = h
         for k, g in enumerate((gg[:unit], gg[unit:], gw)):
             tot[k, units, :] = g if first else tot[k, units, :] + g
 
@@ -169,11 +187,48 @@
         tile = min(256, tokens)
         down = w[pl.ds((block + 1) * chunks, chunks), 2].reshape(chunks * unit, dim)
         for start in range(0, tokens, tile):
-            fo[block, start:start + tile] = dot_tn(hid[:, start:start + tile], down).astype(bf16)
-        pltpu.make_async_copy(fo.at[block], out_hbm.at[block], o_sem.at[block]).start()
+            fo[block, start:start + tile] = dot_tn(hid[block, :, start:start + tile], down).astype(bf16)
+        pltpu.make_async_copy(fo.at[block], out_hbm.at[0, block], o_sem.at[block]).start()
+
+    places = []
+    qo, lo = 0, 0
+    for k, (bit, how, q2, w2) in enumerate(stages):
+        side, _ = partners[k]
+        if how == "lane":
+            give = (qo, lo + (1 - side) * w2)
+            lo = lo + side * w2
+        else:
+            give = (qo + (1 - side) * q2, lo)
+            qo = qo + side * q2
+        places.append((qo, lo, give, q2, w2))
+
+    def region(p, uo, ln, k):
+        return (slice(None), pl.ds(pl.multiple_of(p * piece + uo, 16), places[k][3]),
+                pl.ds(pl.multiple_of(ln, 128), places[k][4]))
+
+    def stage_copy(k, p):
+        return pltpu.make_async_remote_copy(
+            src_ref=sb[k].at[p], dst_ref=rb[k].at[p], send_sem=f_send.at[k, p],
+            recv_sem=f_recv.at[k, p], device_id={"seq": partners[k][1]}, device_id_type=MESH)
+
+    def stage_start(k, p):
+        sb[k][p] = tot[region(p, places[k][2][0], places[k][2][1], k)].astype(bf16)
+        stage_copy(k, p).start()
+
+    def stage_end(k, p):
+        stage_copy(k, p).wait()
+        where = region(p, places[k][0], places[k][1], k)
+        tot[where] = tot[where] + rb[k][p].astype(f32)
+
+    def level_copy(k):
+        return pltpu.make_async_remote_copy(
+            src_ref=lev, dst_ref=levr.at[k], send_sem=l_send.at[k], recv_sem=l_recv.at[k],
+            device_id={"seq": partners[k][1]}, device_id_type=MESH)
+
+    lag = jnp.where(mid, 2, 4)
+    each = piece // unit
 
     def step(t, carry):
-        block = t // chunks
         c = lax.rem(t, chunks)
 
         @pl.when(t == chunks - 1)
@@ -181,76 +236,68 @@
             for copy in later_in:
                 copy.wait()
 
-        @pl.when(t >= chunks)
-        def _():
-            arrive(t - chunks)
-        h, gg, gw = parts(t, kv[block], vv[block], rows_ref[block, 0:1])
-        acc[0:2] = gg.reshape(2, unit, dim)
-        acc[2] = gw
-
-        @pl.when(has_out)
-        def _():
-            recv_copy(0, t).wait_recv()
-            acc[...] += rbuf[0, t].astype(f32)
-        sbuf[t] = acc[...].astype(bf16)
-        send_copy(t).start()
-
-        @pl.when(jnp.logical_and(mid, t > 0))
+        @pl.when(t < 2 * chunks)
+        def _():
+            block = t // chunks
+
+            @pl.when(t >= chunks)
+            def _():
+                arrive(t - chunks)
+            h, gg, gw = parts(t, kv[block], vv[block], rows_ref[block, 0:1])
+            acc[0:2] = gg.reshape(2, unit, dim)
+            acc[2] = gw
+
+            @pl.when(has_out)
+            def _():
+                recv_copy(0, t).wait_recv()
+                acc[...] += rbuf[0, t].astype(f32)
+            sbuf[t] = acc[...].astype(bf16)
+            send_copy(t).start()
+
+        @pl.when(jnp.logical_and(mid, jnp.logical_and(t > 0, t <= 2 * chunks)))
         def _():
             finish(t - 1)
 
-        @pl.when(t >= chunks)
+        @pl.when(jnp.logical_and(t >= chunks, t < 2 * chunks))
         def _():
             outer(0, c, True)
+
+        @pl.when(t == 2 * chunks)
+        def _():
+            write_out(0)
+        late = t - chunks - lag
+
+        @pl.when(jnp.logical_and(late >= 0, late < chunks))
+        def _():
+            arrive(chunks + late)
+            outer(1, late, False)
+            p = late // each
+
+            @pl.when(lax.rem(late, each) == each - 1)
+            def _():
+                stage_start(0, p)
+                for k in range(1, ns + 1):
+                    @pl.when(p >= k)
+                    def _():
+                        stage_end(k - 1, p - k)
+                        if k < ns:
+                            stage_start(k, p - k)
         return carry
 
-    lax.fori_loop(0, 2 * chunks, step, 0)
-
-    @pl.when(mid)
-    def _():
-        finish(2 * chunks - 1)
-    write_out(0)
-
-    def last(c, carry):
-        arrive(chunks + c)
-        outer(1, c, False)
-        return carry
-    lax.fori_loop(0, chunks, last, 0)
-
-    qo, lo = 0, 0
-    q, wd = piece, dim
-    places = []
-    for k, (bit, how, q2, w2) in enumerate(stages):
-        side, partner = partners[k]
-        if how == "lane":
-            keep_q, give_q = qo, qo
-            keep_l, give_l = lo + side * w2, lo + (1 - side) * w2
-        else:
-            keep_q, give_q = qo + side * q2, qo + (1 - side) * q2
-            keep_l, give_l = lo, lo
-
-        def region(p, uo, ln, q2=q2, w2=w2):
-            return (slice(None), pl.ds(pl.multiple_of(p * piece + uo, 16), q2), pl.ds(pl.multiple_of(ln, 128), w2))
-        for p in range(n):
-            sb[k][:, p] = tot[region(p, give_q, give_l)].astype(bf16)
-        copy = pltpu.make_async_remote_copy(
-            src_ref=sb[k], dst_ref=rb[k], send_sem=f_send.at[k], recv_sem=f_recv.at[k],
-            device_id={"seq": partner}, device_id_type=MESH)
-        lcopy = pltpu.make_async_remote_copy(
-            src_ref=lev, dst_ref=levr.at[k], send_sem=l_send.at[k], recv_sem=l_recv.at[k],
-            device_id={"seq": partner}, device_id_type=MESH)
-        copy.start()
-        lcopy.start()
-        if k == 0:
+    lax.fori_loop(0, 2 * chunks + 4, step, 0)
+
+    for e in range(n, n + ns):
+        level_copy(e - n).start()
+        if e == n:
             write_out(1)
-        lcopy.wait()
-        lev[...] = jnp.maximum(lev[...], levr[k])
-        copy.wait()
-        for p in range(n):
-            where = region(p, keep_q, keep_l)
-            tot[where] = tot[where] + rb[k][:, p].astype(f32)
-        qo, lo, q, wd = keep_q, keep_l, q2, w2
-        places.append((qo, lo, q, wd))
+        for k in range(1, ns + 1):
+            if 0 <= e - k < n:
+                stage_end(k - 1, e - k)
+                if k < ns:
+                    stage_start(k, e - k)
+        level_copy(e - n).wait()
+        lev[...] = jnp.maximum(lev[...], levr[e - n])
+    q, wd = places[-1][3], places[-1][4]
 
     for p in range(n):
         zs[p] = tot[:, pl.ds(pl.multiple_of(p * piece + qo, 16), q), pl.ds(pl.multiple_of(lo, 128), wd)].astype(bf16)
@@ -272,17 +319,22 @@
     for d in range(1, n):
         total = total + zr[d - 1].astype(f32)
         top = jnp.maximum(top, levr[ns + d - 1])
-    level_ref[...] = top
+    lev[...] = top
+    for block in range(2):
+        for j in range(each):
+            level_ref[block:block + 1, j * unit:(j + 1) * unit] = lev[block * chunks + me * each + j]
     gat[:, pl.ds(pl.multiple_of(qo, 16), q), pl.ds(pl.multiple_of(lo, 128), wd)] = total.astype(bf16)
     for k in range(ns - 1, -1, -1):
-        uo, ln, q2, w2 = places[k]
+        uo, ln, _, q2, w2 = places[k]
         mine = gat.at[:, pl.ds(pl.multiple_of(uo, 16), q2), pl.ds(pl.multiple_of(ln, 128), w2)]
         copy = pltpu.make_async_remote_copy(
             src_ref=mine, dst_ref=mine, send_sem=g_send.at[k], recv_sem=g_recv.at[k],
             device_id={"seq": partners[k][1]}, device_id_type=MESH)
         copy.start()
         copy.wait()
-    grad_ref[...] = gat[...].astype(f32)
+    gate_out[...] = gat[0].astype(f32).T
+    up_out[...] = gat[1].astype(f32).T
+    down_out[...] = gat[2].astype(f32)
 
     def drain(t, carry):
         send_copy(t).wait_send()
@@ -293,7 +345,7 @@
         return carry
     lax.fori_loop(0, 2 * chunks, drain, 0)
     for block in range(2):
-        pltpu.make_async_copy(fo.at[block], out_hbm.at[block], o_sem.at[block]).wait()
+        pltpu.make_async_copy(fo.at[block], out_hbm.at[0, block], o_sem.at[block]).wait()
 
 
 def per_device(
@@ -305,60 +357,56 @@
     width = w_gate.shape[1]
     n = lax.axis_size("tok")
     nseq = lax.axis_size("seq")
-    where = lax.axis_index("tok")
     piece = width // n
     unit = min(64, piece)
     chunks = width // unit
     stages, q, wd = plan_stages(nseq, piece, dim)
     ns = len(stages)
-    positions = where * rows + jnp.arange(rows, dtype=jnp.int32)
-    count = valid_count[0][:, None]
-    mask = (positions[None] < count).astype(f32)
-    factor = -(loss_scale[0] * token_rate[0] * mask / count.astype(f32))
-    lanes = jnp.stack([factor, mask], axis=1)
-    weights = jnp.stack([w_gate.T, w_up.T, w_down])
-    weights = weights.reshape(3, chunks, unit, dim).transpose(1, 0, 2, 3)
     any_spec = pl.BlockSpec(memory_space=pl.ANY)
     vmem = pl.BlockSpec(memory_space=pltpu.VMEM)
     dma = pltpu.SemaphoreType.DMA
     scratch = [
         pltpu.VMEM((blocks, rows, dim), bf16), pltpu.VMEM((blocks, rows, dim), bf16),
         pltpu.VMEM((blocks, rows, dim), bf16), pltpu.VMEM((blocks, rows, dim), bf16),
+        pltpu.VMEM((3, dim, width), bf16),
+        pltpu.VMEM((blocks, 2, rows), f32),
         pltpu.VMEM((3 * chunks, 3, unit, dim), bf16),
         pltpu.VMEM((2 * chunks, 3, unit, dim), bf16),
         pltpu.VMEM((2, 2 * chunks, 3, unit, dim), bf16),
         pltpu.VMEM((chunks, 3, unit, dim), f32), pltpu.VMEM((chunks, 3, unit, dim), f32),
         pltpu.VMEM((3, unit, dim), f32),
         pltpu.VMEM((3, width, dim), f32),
-        pltpu.VMEM((width, rows), bf16),
+        pltpu.VMEM((blocks, width, rows), bf16),
         pltpu.VMEM((blocks, rows, dim), bf16),
         pltpu.VMEM((2 * chunks, 1, unit), f32),
         pltpu.VMEM((ns + n - 1, 2 * chunks, 1, unit), f32),
         pltpu.VMEM((n, 3, q, wd), bf16), pltpu.VMEM((n - 1, 3, q, wd), bf16),
         pltpu.VMEM((3, piece, dim), bf16),
     ]
-    scratch += [pltpu.VMEM((3, n, a, b), bf16) for _, _, a, b in stages] * 2
+    scratch += [pltpu.VMEM((n, 3, a, b), bf16) for _, _, a, b in stages] * 2
     scratch += [
-        dma((7,)), dma((2 * chunks,)), dma((2, 2 * chunks)), dma((2 * chunks,)), dma((2 * chunks,)),
-        dma((2,)), dma((ns,)), dma((ns,)), dma((ns,)), dma((ns,)), dma((ns,)), dma((ns,)),
+        dma((9,)), dma((2 * chunks,)), dma((2, 2 * chunks)), dma((2 * chunks,)), dma((2 * chunks,)),
+        dma((2,)), dma((ns, n)), dma((ns, n)), dma((ns,)), dma((ns,)), dma((ns,)), dma((ns,)),
         dma((n - 1,)), dma((n - 1,)), dma((n - 1,)), dma((n - 1,)),
     ]
-    fast_out, grads, levels = pl.pallas_call(
+    smem = pl.BlockSpec(memory_space=pltpu.SMEM)
+    return pl.pallas_call(
         functools.partial(kernel, n, nseq, chunks, unit, stages),
         out_shape=(
-            jax.ShapeDtypeStruct((blocks, rows, dim), bf16),
-            jax.ShapeDtypeStruct((3, piece, dim), f32),
-            jax.ShapeDtypeStruct((2 * chunks, 1, unit), f32),
+            jax.ShapeDtypeStruct((1, blocks, rows, dim), bf16),
+            jax.ShapeDtypeStruct((dim, piece), f32),
+            jax.ShapeDtypeStruct((dim, piece), f32),
+            jax.ShapeDtypeStruct((piece, dim), f32),
+            jax.ShapeDtypeStruct((blocks, piece), f32),
         ),
-        in_specs=[pl.BlockSpec(memory_space=pltpu.SMEM)] + [any_spec] * 5 + [vmem],
-        out_specs=(any_spec, vmem, vmem),
+        in_specs=[smem] * 2 + [any_spec] * 7 + [vmem],
+        out_specs=(any_spec, vmem, vmem, vmem, vmem),
         scratch_shapes=scratch,
         compiler_params=pltpu.CompilerParams(
             collective_id=0, has_side_effects=True, vmem_limit_bytes=60 * 2**20
         ),
-    )(loss_scale, keys[0], values[0], queries[0], out_cotangent[0], weights, lanes)
-    levels = lax.dynamic_slice_in_dim(levels.reshape(blocks, width), where * piece, piece, 1)
-    return (fast_out[None], grads[0].T, grads[1].T, grads[2], levels)
+    )(loss_scale, valid_count, keys[0], values[0], queries[0], out_cotangent[0],
+      w_gate, w_up, w_down, token_rate)
 
 
 def solution(mesh):

time: 142 us -> 124 us (0.87)
  Pallas kernels: 126 us -> 117 us
  other arithmetic: 6.24 us -> 0 us
  local copies, waits for them, and re-layouts: 8.52 us -> 5.8 us
    pallas_call x1, Pallas kernels: 126 us -> 117 us  [per_device(): pl.pallas_call(functools.partial(kernel, n, nseq, chunks, unit, stages),...]
    unnamed x7 -> x13, local copies, waits for them, and re-layouts: 3 us -> 5.8 us
    transpose x2 -> x0, local copies, waits for them, and re-layouts: 2.51 us -> none  [per_device(): weights = jnp.stack([w_gate.T, w_up.T, w_down])]
    squeeze x1 -> x0, local copies, waits for them, and re-layouts: 1.86 us -> none  [per_device(): return (fast_out[None], grads[0].T, grads[1].T, grads[2], levels)]
    pallas_call x1 -> x0, other arithmetic: 1.48 us -> none  [per_device(): pl.pallas_call(functools.partial(kernel, n, nseq, chunks, unit, stages),...]
where the time goes in v2:
time: 124 us
  Pallas kernels  117 us (94%)
  local copies, waits for them, and re-layouts  5.8 us (5%)
  between operations  1.32 us (1%)
    pallas_call x1, Pallas kernels, per_device(): pl.pallas_call(functools.partial(kernel, n, nseq, chunks, unit, stages),...  117 us
    unnamed x13, local copies, waits for them, and re-layouts  5.8 us

profile of v2, /device:TPU:0, one launch (start us, length us, event | category | flops | bytes accessed | tf_op | source)
XLA Modules:
  0.0 124.1 jit_solution(6173134959052384569)
XLA Ops:
  1.3 117.0 %shard_map.137 = (bf16[1,2,1024,512]{3,2,1,0:T(8,128)(2,1)}, f32[512,128]{1,0:T(8,128)}, f32[512,128]{1,0:T(8,128)}, f32[128,512]{1,0:T(8,128)}, f32[2,128]{1,0:T(2,128)}) custom-call(f32[1]{0:T(128)S(6)} %copy.20.scale_ref, s32[1,2]{1,0:T(1,128)} %count_ref.1, bf16[2,1024,512]{2,1,0:T(8,128)(2,1)} %bitcast.4, bf16[2,1024,512]{2,1,0:T(8,128)(2,1)} %bitcast.5, ...), custom_call_target="tpu_custom_call" | custom-call | tf_op jit(solution)/shard_map/pallas_call | solution.py:393
  118.3 0.0 copy-start.2
  118.3 0.0 copy-start.1
  118.3 0.0 copy-start
  118.3 0.0 copy-start.3
  118.3 3.1 %copy.21 = bf16[1,2,1024,512]{3,2,1,0:T(8,128)(2,1)} copy(bf16[1,2,1024,512]{3,2,1,0:T(8,128)(2,1)} %get-tuple-element.10) | data formatting | bytes 4194304
  121.4 0.0 copy-done.2
  121.4 0.7 copy.22
  122.1 0.0 copy-done.1
  122.1 0.7 copy.23
  122.8 0.0 copy-done
  122.8 0.7 copy.24
  123.5 0.0 copy-done.3
  123.5 0.6 copy.25
Async XLA Ops:
  118.3 3.2 %copy-start.2 = (f32[512,128]{1,0:T(8,128)S(1)}, f32[512,128]{1,0:T(8,128)}, u32[]{:S(2)}) copy-start(f32[512,128]{1,0:T(8,128)} %get-tuple-element.11) | copy-start | bytes 786436
  118.3 3.9 %copy-start.1 = (f32[512,128]{1,0:T(8,128)S(1)}, f32[512,128]{1,0:T(8,128)}, u32[]{:S(2)}) copy-start(f32[512,128]{1,0:T(8,128)} %get-tuple-element.12) | copy-start | bytes 786436
  118.3 4.5 %copy-start = (f32[128,512]{1,0:T(8,128)S(1)}, f32[128,512]{1,0:T(8,128)}, u32[]{:S(2)}) copy-start(f32[128,512]{1,0:T(8,128)} %get-tuple-element.13) | copy-start | bytes 786436
  118.3 5.2 %copy-start.3 = (f32[2,128]{1,0:T(2,128)S(1)}, f32[2,128]{1,0:T(2,128)}, u32[]{:S(2)}) copy-start(f32[2,128]{1,0:T(2,128)} %get-tuple-element.14) | copy-start | bytes 3076

commit v3 on v2

--- a/solution.py
+++ b/solution.py
@@ -254,17 +254,18 @@
             sbuf[t] = acc[...].astype(bf16)
             send_copy(t).start()
 
+        @pl.when(jnp.logical_and(t >= chunks, t < 2 * chunks))
+        def _():
+            outer(0, c, True)
+
+        @pl.when(t == 2 * chunks)
+        def _():
+            write_out(0)
+
         @pl.when(jnp.logical_and(mid, jnp.logical_and(t > 0, t <= 2 * chunks)))
         def _():
             finish(t - 1)
 
-        @pl.when(jnp.logical_and(t >= chunks, t < 2 * chunks))
-        def _():
-            outer(0, c, True)
-
-        @pl.when(t == 2 * chunks)
-        def _():
-            write_out(0)
         late = t - chunks - lag
 
         @pl.when(jnp.logical_and(late >= 0, late < chunks))

time: 124 us -> 121 us (0.976)
  Pallas kernels: 117 us -> 114 us
    pallas_call x1, Pallas kernels: 117 us -> 114 us  [per_device(): pl.pallas_call(functools.partial(kernel, n, nseq, chunks, unit, stages),...]
where the time goes in v3:
time: 121 us
  Pallas kernels  114 us (94%)
  local copies, waits for them, and re-layouts  5.8 us (5%)
  between operations  1.32 us (1%)
    pallas_call x1, Pallas kernels, per_device(): pl.pallas_call(functools.partial(kernel, n, nseq, chunks, unit, stages),...  114 us
    unnamed x13, local copies, waits for them, and re-layouts  5.8 us

profile of v3, /device:TPU:0, one launch (start us, length us, event | category | flops | bytes accessed | tf_op | source)
XLA Modules:
  0.0 120.7 jit_solution(13497662129375704721)
XLA Ops:
  1.3 113.6 %shard_map.137 = (bf16[1,2,1024,512]{3,2,1,0:T(8,128)(2,1)}, f32[512,128]{1,0:T(8,128)}, f32[512,128]{1,0:T(8,128)}, f32[128,512]{1,0:T(8,128)}, f32[2,128]{1,0:T(2,128)}) custom-call(f32[1]{0:T(128)S(6)} %copy.20.scale_ref, s32[1,2]{1,0:T(1,128)} %count_ref.1, bf16[2,1024,512]{2,1,0:T(8,128)(2,1)} %bitcast.4, bf16[2,1024,512]{2,1,0:T(8,128)(2,1)} %bitcast.5, ...), custom_call_target="tpu_custom_call" | custom-call | tf_op jit(solution)/shard_map/pallas_call | solution.py:394
  114.9 0.0 copy-start.2
  114.9 0.0 copy-start.1
  114.9 0.0 copy-start
  114.9 0.0 copy-start.3
  114.9 3.1 %copy.21 = bf16[1,2,1024,512]{3,2,1,0:T(8,128)(2,1)} copy(bf16[1,2,1024,512]{3,2,1,0:T(8,128)(2,1)} %get-tuple-element.10) | data formatting | bytes 4194304
  118.0 0.0 copy-done.2
  118.0 0.7 copy.22
  118.7 0.0 copy-done.1
  118.7 0.7 copy.23
  119.5 0.0 copy-done
  119.5 0.7 copy.24
  120.2 0.0 copy-done.3
  120.2 0.6 copy.25
Async XLA Ops:
  114.9 3.2 %copy-start.2 = (f32[512,128]{1,0:T(8,128)S(1)}, f32[512,128]{1,0:T(8,128)}, u32[]{:S(2)}) copy-start(f32[512,128]{1,0:T(8,128)} %get-tuple-element.11) | copy-start | bytes 786436
  114.9 3.9 %copy-start.1 = (f32[512,128]{1,0:T(8,128)S(1)}, f32[512,128]{1,0:T(8,128)}, u32[]{:S(2)}) copy-start(f32[512,128]{1,0:T(8,128)} %get-tuple-element.12) | copy-start | bytes 786436
  114.9 4.5 %copy-start = (f32[128,512]{1,0:T(8,128)S(1)}, f32[128,512]{1,0:T(8,128)}, u32[]{:S(2)}) copy-start(f32[128,512]{1,0:T(8,128)} %get-tuple-element.13) | copy-start | bytes 786436
  114.9 5.2 %copy-start.3 = (f32[2,128]{1,0:T(2,128)S(1)}, f32[2,128]{1,0:T(2,128)}, u32[]{:S(2)}) copy-start(f32[2,128]{1,0:T(2,128)} %get-tuple-element.14) | copy-start | bytes 3076
